TPU v7x, 256 devices: a whole 4x4x8 slice. The times are simulated.
256 devices in a mesh: frame: 32 (over z, x), head: 8 (over y, core).
Axes of the slice: x: 4, y: 4, z: 8, core: 2. Of those that a mesh axis runs over, the one named last changes fastest.
Arguments:
- qkv: bfloat16 [32768, 3, 3072], P('frame', None, 'head'), may hold values from -24 to 24
- head_kinds: int32 [24], replicated, may hold values from 0 to 1
- out_weight: bfloat16 [3072, 3072], P('head'), may hold values from -0.375 to 0.375
Outputs:
- projected: bfloat16 [32768, 3072], P('frame', 'head')
All inputs are finite; a program needn't handle non-finite values.
Results may differ from a plain program's by a relative error of at most 0.017.
Values may be sent and summed in bfloat16 or wider, within the bound.
A program may use at most 64 MiB of HBM per device.

v0:
```python
import jax
import jax.numpy as jnp
from jax import lax
from jax.sharding import PartitionSpec as P

HD = 128


def broadcast(array, axis, root):
    mine = lax.axis_index(axis) == root
    return lax.psum(jnp.where(mine, array, jnp.zeros_like(array)), axis)


def attend(queries, key_rows, value_rows, usable):
    scale = queries.shape[-1] ** (-0.5)
    scores = jnp.dot(queries, key_rows.T, preferred_element_type=jnp.float32) * scale
    scores = jnp.where(usable, scores, -1e30)
    row_max = jnp.max(scores, axis=-1, keepdims=True)
    expo = jnp.exp(scores - row_max)
    normalizer = jnp.sum(expo, axis=-1, keepdims=True)
    weights = expo.astype(jnp.bfloat16)
    return (jnp.dot(weights, value_rows, preferred_element_type=jnp.float32) / normalizer).astype(
        jnp.bfloat16
    )


def across_frames(gathered):
    scale = gathered.shape[-1] ** (-0.5)
    query_part = gathered[:, :, 0]
    key_part = gathered[:, :, 1]
    value_part = gathered[:, :, 2]
    scores = (
        jnp.einsum("fpnd,gpnd->pnfg", query_part, key_part, preferred_element_type=jnp.float32)
        * scale
    )
    row_max = jnp.max(scores, axis=-1, keepdims=True)
    expo = jnp.exp(scores - row_max)
    normalizer = jnp.sum(expo, axis=-1)
    weights = expo.astype(jnp.bfloat16)
    mixed = jnp.einsum("pnfg,gpnd->fpnd", weights, value_part, preferred_element_type=jnp.float32)
    mixed = (mixed / normalizer.transpose(2, 0, 1)[:, :, :, None]).astype(jnp.bfloat16)
    return lax.all_to_all(mixed, "frame", split_axis=0, concat_axis=1, tiled=True)


def local(qkv, head_kinds, out_weight):
    tok_rows = qkv.shape[0]
    local_width = qkv.shape[2]
    heads_here = local_width // HD
    kinds_here = lax.dynamic_slice_in_dim(
        head_kinds, lax.axis_index("head") * heads_here, heads_here
    )
    first_frame_kv = broadcast(qkv[:, 1:, :], "frame", 0)
    arranged = qkv.reshape(1, tok_rows, 3, heads_here, HD)
    temporal_out = across_frames(
        lax.all_to_all(arranged, "frame", split_axis=1, concat_axis=0, tiled=True)
    )
    temporal_out = temporal_out.reshape(tok_rows, heads_here, HD)
    is_first = lax.axis_index("frame") == 0
    block_rows = min(512, tok_rows)
    block_count = tok_rows // block_rows
    column = jnp.arange(2 * tok_rows, dtype=jnp.int32)
    usable = ((column < tok_rows) | jnp.logical_not(is_first))[None, :]
    attended_heads = []
    for head_slot in range(heads_here):
        col_start = head_slot * HD
        key_rows = jnp.concatenate(
            [
                qkv[:, 1, col_start : col_start + HD],
                first_frame_kv[:, 0, col_start : col_start + HD],
            ],
            axis=0,
        )
        value_rows = jnp.concatenate(
            [
                qkv[:, 2, col_start : col_start + HD],
                first_frame_kv[:, 1, col_start : col_start + HD],
            ],
            axis=0,
        )
        query_rows = qkv[:, 0, col_start : col_start + HD]

        def spatial_head(query_rows=query_rows, key_rows=key_rows, value_rows=value_rows):
            query_blocks = query_rows.reshape(block_count, block_rows, HD)
            outcome = lax.map(
                lambda query_block: attend(query_block, key_rows, value_rows, usable), query_blocks
            )
            return outcome.reshape(tok_rows, HD)

        def temporal_head(head_slot=head_slot):
            return temporal_out[:, head_slot, :]

        attended_heads.append(lax.cond(kinds_here[head_slot] == 1, temporal_head, spatial_head))
    attended = jnp.concatenate(attended_heads, axis=1)
    partial_term = jnp.dot(attended, out_weight, preferred_element_type=jnp.float32)
    summed = lax.psum_scatter(
        partial_term.astype(jnp.bfloat16), "head", scatter_dimension=1, tiled=True
    )
    return summed


def solution(mesh):
    placed = (P("frame", None, "head"), P(), P("head", None))
    return jax.shard_map(
        local, mesh=mesh, in_specs=placed, out_specs=P("frame", "head"), check_vma=False
    )
```

profile of v0, /device:TPU:1, one launch (start us, length us, event | category | flops | bytes accessed | tf_op | source)
XLA Modules:
  0.0 312.5 jit_solution(17163701035604100749)
XLA Ops:
  6.5 4.4 %copy.39 = bf16[1024,3,384]{0,2,1:T(8,128)(2,1)} copy(bf16[1024,3,384]{2,0,1:T(8,128)(2,1)} %param.15) | data formatting | bytes 4718592 | tf_op args[0]
  11.0 5.8 %copy.40 = bf16[1,1024,3,3,128]{4,3,2,0,1:T(4,128)(2,1)} copy(bf16[1,1024,3,3,128]{1,4,3,2,0:T(8,128)(2,1)} %bitcast.125) | data formatting | bytes 4718592 | tf_op jit(solution)/shard_map/reshape | solution.py:53
  16.7 12.1 %all-to-all-start = ((bf16[1,1024,3,3,128]{4,3,2,0,1:T(4,128)(2,1)}), bf16[1,1024,3,3,128]{4,3,2,0,1:T(4,128)(2,1)}, u32[]{:S(2)}, u32[]{:S(2)}) async-start(bf16[1,1024,3,3,128]{4,3,2,0,1:T(4,128)(2,1)} %copy.40), calls=%async_computation | async-start | bytes 6291456 | tf_op jit(solution)/shard_map/all_to_all | solution.py:55
  28.9 2.8 slice_select_fusion
  31.8 77.2 %all-to-all-done = bf16[1,1024,3,3,128]{4,3,2,0,1:T(4,128)(2,1)} async-done(((bf16[1,1024,3,3,128]{4,3,2,0,1:T(4,128)(2,1)}), bf16[1,1024,3,3,128]{4,3,2,0,1:T(4,128)(2,1)}, u32[]{:S(2)}, u32[]{:S(2)}) %all-to-all-start) | async-done | bytes 2359328 | tf_op jit(solution)/shard_map/all_to_all | solution.py:55
  109.1 2.2 copy.41
  113.2 1.3 fusion.72
  114.5 1.2 copy.46
  115.7 8.1 %all-to-all-start.1 = ((bf16[32,32,3,128]{3,1,2,0:T(8,128)(2,1)}), bf16[32,32,3,128]{3,1,2,0:T(8,128)(2,1)}, u32[]{:S(2)}, u32[]{:S(2)}) async-start(bf16[32,32,3,128]{3,1,2,0:T(8,128)(2,1)} %copy.46), calls=%async_computation.1 | async-start | bytes 1572864 | tf_op jit(solution)/shard_map/all_to_all | solution.py:42
  126.4 2.4 slice_bitcast_fusion.10
  128.8 75.2 %all-reduce.2.cloned.1.call-done = bf16[1024,2,384]{2,0,1:T(8,128)(2,1)} async-done(((bf16[1024,2,384]{2,0,1:T(8,128)(2,1)}), bf16[1024,2,384]{2,0,1:T(8,128)(2,1)}) %all-reduce.2.cloned.1.call-update) | async-done | bytes 1572880 | tf_op jit(solution)/shard_map/psum | solution.py:11
  204.0 1.5 slice_bitcast_fusion.4
  205.5 1.9 pad_maximum_fusion
  207.4 1.1 pad_maximum_fusion.4
  209.3 1.2 copy.47
  210.5 1.6 copy.48
  212.1 11.2 %conditional.5 = (bf16[1024,128]{1,0:T(8,128)(2,1)}) conditional(s32[]{:T(128)} %bitcast.33, (bf16[1024,3,384]{2,0,1:T(8,128)(2,1)}, pred[1,2048]{1,0:T(4,128)(4,1)S(1)}, bf16[2048,128]{1,0:T(8,128)(2,1)}, bf16[2048,128]{1,0:T(8,128)(2,1)}) %tuple.37, bf16[1024,3,128]{2,1,0:T(4,128)(2,1)} %copy.48), branch_computations={%region_15.20_spmd, %region_20.21_spmd} | conditional | flops 548535296 | bytes 18632968 | solution.py:92
  212.1 1.7 slice.57
  213.8 9.6 %while.29 = (s32[]{:T(128)}, bf16[2,512,128]{2,1,0:T(8,128)(2,1)}, pred[1,2048]{1,0:T(4,128)(4,1)S(1)}, bf16[2,512,128]{2,1,0:T(8,128)(2,1)}, bf16[2048,128]{1,0...) while((s32[]{:T(128)}, bf16[2,512,128]{2,1,0:T(8,128)(2,1)}, ...), condition=%wide.region_19.19_spmd, body=%wide.region_16.18_spmd.sunk | while | flops 548535296 | bytes 18108600 | solution.py:84
  213.9 2.0 fusion.114
  218.6 2.0 fusion.114
  223.4 10.9 %conditional.4 = (bf16[1024,128]{1,0:T(8,128)(2,1)}) conditional(s32[]{:T(128)} %bitcast.28, (bf16[1024,3,384]{2,0,1:T(8,128)(2,1)}, pred[1,2048]{1,0:T(4,128)(4,1)S(1)}, bf16[2048,128]{1,0:T(8,128)(2,1)S(1)}, bf16[2048,128]{1,0:T(8,128)(2,1)}) %tuple.36, bf16[1024,3,128]{2,1,0:T(4,128)(2,1)} %copy.48), branch_computations={%region_9.14_spmd, %region_14.15_spmd} | conditional | flops 548535296 | bytes 18632968 | solution.py:92
  223.4 1.7 slice.55
  225.1 9.2 %while.28 = (s32[]{:T(128)}, bf16[2,512,128]{2,1,0:T(8,128)(2,1)}, pred[1,2048]{1,0:T(4,128)(4,1)S(1)}, bf16[2,512,128]{2,1,0:T(8,128)(2,1)}, bf16[2048,128]{1,0...) while((s32[]{:T(128)}, bf16[2,512,128]{2,1,0:T(8,128)(2,1)}, ...), condition=%wide.region_13.13_spmd, body=%wide.region_10.12_spmd.sunk | while | flops 548535296 | bytes 18108600 | solution.py:84
  225.1 1.8 fusion.120
  229.7 1.8 fusion.120
  234.2 8.3 %conditional.3 = (bf16[1024,128]{1,0:T(8,128)(2,1)}) conditional(s32[]{:T(128)} %bitcast.15, (bf16[1024,3,384]{2,0,1:T(8,128)(2,1)}, pred[1,2048]{1,0:T(4,128)(4,1)S(1)}, bf16[2048,128]{1,0:T(8,128)(2,1)S(1)}, bf16[2048,128]{1,0:T(8,128)(2,1)}) %tuple.35, bf16[1024,3,128]{2,1,0:T(4,128)(2,1)} %copy.48), branch_computations={%region_3.8_spmd, %region_8.9_spmd} | conditional | flops 548535296 | bytes 18632968 | solution.py:92
  235.2 7.3 %while.27 = (s32[]{:T(128)}, bf16[2,512,128]{2,1,0:T(8,128)(2,1)}, pred[1,2048]{1,0:T(4,128)(4,1)S(1)}, bf16[2,512,128]{2,1,0:T(8,128)(2,1)S(1)}, bf16[2048,128]...) while((s32[]{:T(128)}, bf16[2,512,128]{2,1,0:T(8,128)(2,1)}, ...), condition=%wide.region_7.7_spmd, body=%wide.region_4.6_spmd.sunk | while | flops 548535296 | bytes 18108600 | solution.py:84
  242.5 6.5 %convolution_convert_fusion = bf16[1024,3072]{1,0:T(8,128)(2,1)} fusion(bf16[384,3072]{1,0:T(8,128)(2,1)S(1)} %copy-done, bf16[1024,128]{1,0:T(8,128)(2,1)} %get-tuple-element.417, bf16[1024,128]{1,0:T(8,128)(2,1)} %get-tuple-element.416, bf16[1024,128]{1,0:T(8,128)(2,1)} %get-tuple-element.415), kind=kOutput, calls=%fused_computation.54 | convolution fusion | flops 2421424128 | bytes 9437184 | tf_op jit(solution)/shard_map/dot_general | solution.py:94
  249.0 8.6 %copy.52 = bf16[1024,3072]{0,1:T(8,128)(2,1)} copy(bf16[1024,3072]{1,0:T(8,128)(2,1)} %convolution_convert_fusion) | data formatting | bytes 12582912
  257.7 45.7 %reduce-scatter.4.cloned.1.call-done = bf16[384,1024]{1,0:T(8,128)(2,1)} async-done(((bf16[3072,1024]{1,0:T(8,128)(2,1)}), bf16[384,1024]{1,0:T(8,128)(2,1)}) %reduce-scatter.4.cloned.1.call-update) | async-done | bytes 786448
  303.4 2.3 copy.53
  (80 shorter events, 22.6 us)
Async XLA Ops:
  6.5 236.0 %copy-start = (bf16[384,3072]{1,0:T(8,128)(2,1)S(1)}, bf16[384,3072]{1,0:T(8,128)(2,1)}, u32[]{:S(2)}) copy-start(bf16[384,3072]{1,0:T(8,128)(2,1)} %param.17) | copy-start | bytes 7077892
  16.7 15.0 %copy-start.6 = (s32[24]{0:T(128)S(1)}, s32[24]{0:T(128)}, u32[]{:S(2)}) copy-start(s32[24]{0:T(128)} %param.16) | copy-start | bytes 292
  16.7 92.3 %all-to-all-start = ((bf16[1,1024,3,3,128]{4,3,2,0,1:T(4,128)(2,1)}), bf16[1,1024,3,3,128]{4,3,2,0,1:T(4,128)(2,1)}, u32[]{:S(2)}, u32[]{:S(2)}) async-start(bf16[1,1024,3,3,128]{4,3,2,0,1:T(4,128)(2,1)} %copy.40), calls=%async_computation | async-start | bytes 6291456 | tf_op jit(solution)/shard_map/all_to_all | solution.py:55
  28.9 175.1 %all-reduce.2.cloned.1.call-start = ((), (), s32[]{:S(2)}) async-start(), calls=%async_computation.3 | async-start | bytes 3145728 | tf_op jit(solution)/shard_map/psum | solution.py:11
  115.7 93.6 %all-to-all-start.1 = ((bf16[32,32,3,128]{3,1,2,0:T(8,128)(2,1)}), bf16[32,32,3,128]{3,1,2,0:T(8,128)(2,1)}, u32[]{:S(2)}, u32[]{:S(2)}) async-start(bf16[32,32,3,128]{3,1,2,0:T(8,128)(2,1)} %copy.46), calls=%async_computation.1 | async-start | bytes 1572864 | tf_op jit(solution)/shard_map/all_to_all | solution.py:42
  123.8 179.6 %reduce-scatter.4.cloned.1.call-start = ((), (), s32[]{:S(2)}) async-start(), calls=%async_computation.4 | async-start | bytes 7077888
  203.9 4.5 %copy-start.1 = (bf16[1024,128]{1,0:T(8,128)(2,1)S(1)}, bf16[1024,128]{1,0:T(8,128)(2,1)}, u32[]{:S(2)}) copy-start(bf16[1024,128]{1,0:T(8,128)(2,1)} %get-tuple-element.196) | copy-start | bytes 786436
  204.0 4.5 %copy-start.2 = (bf16[1024,128]{1,0:T(8,128)(2,1)S(1)}, bf16[1024,128]{1,0:T(8,128)(2,1)}, u32[]{:S(2)}) copy-start(bf16[1024,128]{1,0:T(8,128)(2,1)} %get-tuple-element.197) | copy-start | bytes 786436
  213.8 3.0 copy-start.5
  213.8 3.0 copy-start.7
  217.9 0.7 copy-start.8
  218.6 3.0 copy-start.5
  218.6 3.0 copy-start.7
  222.7 0.7 copy-start.8
  225.1 2.8 copy-start.4
  225.1 2.8 copy-start.9
  228.9 0.7 copy-start.10
  229.7 2.8 copy-start.4
  229.7 2.8 copy-start.9
  233.5 0.7 copy-start.10
  235.3 1.8 copy-start.3
  235.3 1.8 copy-start.11
  238.1 0.7 copy-start.12
  238.9 1.8 copy-start.3
  238.9 1.8 copy-start.11
  241.8 0.7 copy-start.12
Sparse Core Ops, SparseCore 0:
  33.1 170.7 all-reduce.1
  257.8 45.5 reduce-scatter.3
where the time goes:
time: 313 us; the launch traced here: 312 us
  waiting for transfers between devices  198 us (63%)
  local copies, waits for them, and re-layouts  41 us (13%)
  matrix products  24.4 us (8%)
  starting transfers between devices  20.3 us (6%)
  between operations  15.4 us (5%)
  other arithmetic  13 us (4%)
    all_to_all x1, waiting for transfers between devices, local(): lax.all_to_all(arranged, 'frame', split_axis=1, concat_axis=0, tiled=True)  77.2 us
    psum x1, waiting for transfers between devices, broadcast(): return lax.psum(jnp.where(mine, array, jnp.zeros_like(array)), axis)  75.2 us
    unnamed x3, waiting for transfers between devices  45.7 us
    unnamed x11, local copies, waits for them, and re-layouts  15.4 us
    all_to_all x1, starting transfers between devices, local(): lax.all_to_all(arranged, 'frame', split_axis=1, concat_axis=0, tiled=True)  12.1 us
    dot_general x6, matrix products, attend(): jnp.dot(queries, key_rows.T, preferred_element_type=jnp.float32) * scale  9.39 us
    all_to_all x1, starting transfers between devices, across_frames(): lax.all_to_all(mixed, 'frame', split_axis=0, concat_axis=1, tiled=True)  8.09 us
    dot_general x1, matrix products, local(): jnp.dot(attended, out_weight, preferred_element_type=jnp.float32)  6.51 us
  transfers between devices with their start and end apart: 4, of which 3 were waited for; matrix products, arithmetic and copies ran while one was open for 6% of the time, Pallas kernels for 0%

commit v1 on v0

v1 whole, which is shorter than its diff:
```python
import functools

import jax
import jax.numpy as jnp
from jax import lax
from jax.experimental import pallas as pl
from jax.experimental.pallas import tpu as pltpu
from jax.sharding import PartitionSpec as P

HD = 128
MESH = pl.DeviceIdType.MESH
NX = 4
NZ = 8
NF = NX * NZ
NY = 4
HL = 3
HC = 2 * HL
TOK = 1024
HALF = TOK // 2
ROWS = HALF // NF
CH = TOK // NF
WL = HL * HD
WC = HC * HD
QB = 256
SCALE = HD ** -0.5


def rdma(src, dst, send_sem, recv_sem, where):
    return pltpu.make_async_remote_copy(
        src_ref=src, dst_ref=dst, send_sem=send_sem, recv_sem=recv_sem,
        device_id=where, device_id_type=MESH,
    )


def dot_t(a, b):
    return lax.dot_general(a, b, (((1,), (1,)), ((), ())), preferred_element_type=jnp.float32)


def dot(a, b):
    return jnp.dot(a, b, preferred_element_type=jnp.float32)


def kernel(
    slots, kinds, qkv, weight, out,
    qkv6, stage, recv, ostage, oret, kv0, satt, att6, att, wfull,
    far_out, far_in, near_out, near_in, swap_out,
    loc_sem, px_send, px_recv, a_send, a_recv, o_send, o_recv,
    sc_send, sc_recv, z_send, z_recv, x_send, x_recv, y_send, y_recv,
):
    me = lax.axis_index("frame")
    mh = lax.axis_index("head")
    z, x = me // NX, me % NX
    y, c = mh // 2, mh % 2
    other = 1 - c
    partner = {"head": y * 2 + other}
    plus = {"head": lax.rem(y + 1, NY) * 2 + c}
    minus = {"head": lax.rem(y + NY - 1, NY) * 2 + c}

    barrier = pltpu.get_barrier_semaphore()

    def greet(j, carry):
        pl.semaphore_signal(
            barrier, inc=1, device_id={"frame": lax.rem(me + j, NF)}, device_id_type=MESH
        )
        return carry

    lax.fori_loop(1, NF, greet, 0)
    for who in (partner, plus, minus):
        pl.semaphore_signal(barrier, inc=1, device_id=who, device_id_type=MESH)

    my_rows = pl.ds(pl.multiple_of(c * HALF, HALF), HALF)
    other_rows = pl.ds(pl.multiple_of(other * HALF, HALF), HALF)
    my_lanes = pl.ds(pl.multiple_of(c * WL, HD), WL)
    other_lanes = pl.ds(pl.multiple_of(other * WL, HD), WL)
    my_wrows = pl.ds(pl.multiple_of(c * WL, HD), WL)

    own_qkv = pltpu.make_async_copy(qkv.at[:, my_rows, :], qkv6.at[:, :, my_lanes], loc_sem.at[0])
    own_qkv.start()
    own_w = pltpu.make_async_copy(weight, wfull.at[my_wrows, :], loc_sem.at[1])
    own_w.start()

    pl.semaphore_wait(barrier, NF - 1 + 3)

    swap = rdma(
        qkv.at[:, other_rows, :], qkv6.at[:, :, my_lanes], px_send.at[0], px_recv.at[0], partner
    )
    swap.start()

    @pl.when(me == 0)
    def _():
        own_chunk = pltpu.make_async_copy(
            qkv.at[pl.ds(1, 2), pl.ds(0, CH), :], kv0.at[:, 0, 0], sc_recv
        )
        own_chunk.start()

        def scatter(j, carry):
            rows = pl.ds(pl.multiple_of(j * CH, CH), CH)
            rdma(
                qkv.at[pl.ds(1, 2), rows, :], kv0.at[:, j // NX, j % NX],
                sc_send.at[j], sc_recv, {"frame": j},
            ).start()
            return carry

        lax.fori_loop(1, NF, scatter, 0)

    swap_w = rdma(weight, wfull.at[my_wrows, :], px_send.at[1], px_recv.at[1], partner)
    swap_w.start()

    own_qkv.wait()
    rdma(
        qkv.at[:, my_rows, :], qkv6.at[:, :, other_lanes], px_send.at[0], px_recv.at[0], partner
    ).wait_recv()

    for t in range(slots):
        for i in range(3):
            stage[:, t, i] = qkv6[i, :, t * HD : (t + 1) * HD].reshape(NF, ROWS, HD)

    def send_parts(j, carry):
        to = lax.rem(me + j, NF)
        rdma(stage.at[to], recv.at[me], a_send.at[to], a_recv.at[me], {"frame": to}).start()
        return carry

    lax.fori_loop(1, NF, send_parts, 0)
    recv[pl.ds(me, 1)] = stage[pl.ds(me, 1)]

    pltpu.make_async_copy(
        qkv.at[pl.ds(1, 2), pl.ds(0, CH), :], kv0.at[:, z, x], sc_recv
    ).wait()

    def send_z(j, carry):
        to = lax.rem(z + j, NZ)
        rdma(
            kv0.at[:, z, x], kv0.at[:, z, x], z_send.at[to], z_recv.at[z], {"frame": to * NX + x}
        ).start()
        return carry

    lax.fori_loop(1, NZ, send_z, 0)

    def wait_z(j, carry):
        at = lax.rem(z + j, NZ)
        rdma(
            kv0.at[:, at, x], kv0.at[:, at, x], z_send.at[at], z_recv.at[at],
            {"frame": at * NX + x},
        ).wait_recv()
        return carry

    lax.fori_loop(1, NZ, wait_z, 0)

    def send_x(j, carry):
        to = lax.rem(x + j, NX)
        rdma(
            kv0.at[:, :, x], kv0.at[:, :, x], x_send.at[to], x_recv.at[x], {"frame": z * NX + to}
        ).start()
        return carry

    lax.fori_loop(1, NX, send_x, 0)

    def wait_x(j, carry):
        at = lax.rem(x + j, NX)
        rdma(
            kv0.at[:, :, at], kv0.at[:, :, at], x_send.at[at], x_recv.at[at],
            {"frame": z * NX + at},
        ).wait_recv()
        return carry

    lax.fori_loop(1, NX, wait_x, 0)

    for h in range(HL):
        lanes = slice(h * HD, (h + 1) * HD)

        def spatial(b, carry, lanes=lanes):
            rows = pl.ds(pl.multiple_of(b * QB, QB), QB)
            q = qkv[0, rows, lanes]
            s_own = dot_t(q, qkv[1, :, lanes]) * SCALE
            s_first = dot_t(q, kv0[0, :, :, :, lanes].reshape(TOK, HD)) * SCALE
            s_first = jnp.where(me == 0, -1e30, s_first)
            top = jnp.maximum(
                jnp.max(s_own, axis=-1, keepdims=True), jnp.max(s_first, axis=-1, keepdims=True)
            )
            e_own = jnp.exp(s_own - top)
            e_first = jnp.exp(s_first - top)
            norm = jnp.sum(e_own, axis=-1, keepdims=True) + jnp.sum(e_first, axis=-1, keepdims=True)
            mixed = dot(e_own.astype(jnp.bfloat16), qkv[2, :, lanes])
            mixed += dot(
                e_first.astype(jnp.bfloat16), kv0[1, :, :, :, lanes].reshape(TOK, HD)
            )
            satt[rows, lanes] = (mixed / norm).astype(jnp.bfloat16)
            return carry

        lax.fori_loop(0, TOK // QB, spatial, 0)

    swap_s = rdma(
        satt.at[other_rows, :], att6.at[:, my_lanes], px_send.at[2], px_recv.at[2], partner
    )
    swap_s.start()
    own_s = pltpu.make_async_copy(satt.at[my_rows, :], att6.at[:, my_lanes], loc_sem.at[2])
    own_s.start()

    def wait_parts(j, carry):
        at = lax.rem(me + NF - j, NF)
        rdma(stage.at[at], recv.at[at], a_send.at[at], a_recv.at[at], {"frame": at}).wait_recv()
        return carry

    lax.fori_loop(1, NF, wait_parts, 0)

    span = NF * ROWS
    same = (
        lax.broadcasted_iota(jnp.int32, (span, span), 0) % ROWS
        == lax.broadcasted_iota(jnp.int32, (span, span), 1) % ROWS
    )

    def temporal(t, carry):
        q = recv[:, t, 0].reshape(span, HD)
        k = recv[:, t, 1].reshape(span, HD)
        v = recv[:, t, 2].reshape(span, HD)
        s = jnp.where(same, dot_t(q, k) * SCALE, -1e30)
        e = jnp.exp(s - jnp.max(s, axis=-1, keepdims=True))
        norm = jnp.sum(e, axis=-1, keepdims=True)
        o = dot(e.astype(jnp.bfloat16), v) / norm
        ostage[:, t] = o.astype(jnp.bfloat16).reshape(NF, ROWS, HD)
        return carry

    lax.fori_loop(0, slots, temporal, 0)

    def send_back(j, carry):
        to = lax.rem(me + j, NF)
        rdma(ostage.at[to], oret.at[me], o_send.at[to], o_recv.at[me], {"frame": to}).start()
        return carry

    lax.fori_loop(1, NF, send_back, 0)
    oret[pl.ds(me, 1)] = ostage[pl.ds(me, 1)]

    own_s.wait()
    rdma(
        satt.at[my_rows, :], att6.at[:, other_lanes], px_send.at[2], px_recv.at[2], partner
    ).wait_recv()
    own_w.wait()
    rdma(
        weight, wfull.at[pl.ds(pl.multiple_of(other * WL, HD), WL), :],
        px_send.at[1], px_recv.at[1], partner,
    ).wait_recv()

    def wait_back(j, carry):
        at = lax.rem(me + NF - j, NF)
        rdma(ostage.at[at], oret.at[at], o_send.at[at], o_recv.at[at], {"frame": at}).wait_recv()
        return carry

    lax.fori_loop(1, NF, wait_back, 0)

    for h in range(HC):
        lanes = slice(h * HD, (h + 1) * HD)
        is_temporal = kinds[y * HC + h] == 1
        att[:, lanes] = jnp.where(
            is_temporal, oret[:, h].reshape(HALF, HD), att6[:, lanes]
        )

    def product(block, half):
        start = pl.multiple_of(block * WC + half * WL, HD)
        return dot(att[...], wfull[:, pl.ds(start, WL)])

    up, down, far = lax.rem(y + 1, NY), lax.rem(y + NY - 1, NY), lax.rem(y + 2, NY)
    sends = []

    def send(src, dst, index, who):
        copy = rdma(src, dst, y_send.at[index], y_recv.at[index], who)
        copy.start()
        sends.append(copy)

    far_out[0] = product(far, 0).astype(jnp.bfloat16)
    send(far_out.at[0], far_in.at[0], 0, plus)
    far_out[1] = product(far, 1).astype(jnp.bfloat16)
    send(far_out.at[1], far_in.at[1], 1, minus)
    near_out[0, 1] = product(up, 1).astype(jnp.bfloat16)
    send(near_out.at[0, 1], near_in.at[0, 1], 2, plus)
    near_out[1, 0] = product(down, 0).astype(jnp.bfloat16)
    send(near_out.at[1, 0], near_in.at[1, 0], 3, minus)
    up_part = product(up, 0)
    sends[0].wait_recv()
    near_out[0, 0] = (up_part + far_in[0].astype(jnp.float32)).astype(jnp.bfloat16)
    send(near_out.at[0, 0], near_in.at[0, 0], 4, plus)
    down_part = product(down, 1)
    sends[1].wait_recv()
    near_out[1, 1] = (down_part + far_in[1].astype(jnp.float32)).astype(jnp.bfloat16)
    send(near_out.at[1, 1], near_in.at[1, 1], 5, minus)

    for index in range(2, 6):
        sends[index].wait_recv()

    def total(half):
        return (
            product(y, half)
            + near_in[0, half].astype(jnp.float32)
            + near_in[1, half].astype(jnp.float32)
        ).astype(jnp.bfloat16)

    swap_out[...] = total(other)
    last = rdma(swap_out, out.at[my_rows, :], px_send.at[3], px_recv.at[3], partner)
    last.start()
    out[my_rows, :] = total(c)
    rdma(swap_out, out.at[other_rows, :], px_send.at[3], px_recv.at[3], partner).wait_recv()

    swap.wait_send()
    swap_w.wait_send()
    swap_s.wait_send()
    last.wait_send()
    for copy in sends:
        copy.wait_send()

    def drain(j, carry):
        to = lax.rem(me + j, NF)
        rdma(stage.at[to], recv.at[me], a_send.at[to], a_recv.at[me], {"frame": to}).wait_send()
        rdma(ostage.at[to], oret.at[me], o_send.at[to], o_recv.at[me], {"frame": to}).wait_send()
        return carry

    lax.fori_loop(1, NF, drain, 0)

    def drain_z(j, carry):
        to = lax.rem(z + j, NZ)
        rdma(
            kv0.at[:, z, x], kv0.at[:, z, x], z_send.at[to], z_recv.at[z], {"frame": to * NX + x}
        ).wait_send()
        return carry

    lax.fori_loop(1, NZ, drain_z, 0)

    def drain_x(j, carry):
        to = lax.rem(x + j, NX)
        rdma(
            kv0.at[:, :, x], kv0.at[:, :, x], x_send.at[to], x_recv.at[x], {"frame": z * NX + to}
        ).wait_send()
        return carry

    lax.fori_loop(1, NX, drain_x, 0)

    @pl.when(me == 0)
    def _():
        def drain_s(j, carry):
            rows = pl.ds(pl.multiple_of(j * CH, CH), CH)
            rdma(
                qkv.at[pl.ds(1, 2), rows, :], kv0.at[:, j // NX, j % NX],
                sc_send.at[j], sc_recv, {"frame": j},
            ).wait_send()
            return carry

        lax.fori_loop(1, NF, drain_s, 0)


def attention(slots, kinds, qkv, weight):
    bf = jnp.bfloat16
    vmem = pl.BlockSpec(memory_space=pltpu.VMEM)
    dma = pltpu.SemaphoreType.DMA
    return pl.pallas_call(
        functools.partial(kernel, slots),
        out_shape=jax.ShapeDtypeStruct((TOK, WL), bf),
        in_specs=[pl.BlockSpec(memory_space=pltpu.SMEM), vmem, vmem],
        out_specs=vmem,
        scratch_shapes=[
            pltpu.VMEM((3, HALF, WC), bf),
            pltpu.VMEM((NF, slots, 3, ROWS, HD), bf),
            pltpu.VMEM((NF, slots, 3, ROWS, HD), bf),
            pltpu.VMEM((NF, slots, ROWS, HD), bf),
            pltpu.VMEM((NF, slots, ROWS, HD), bf),
            pltpu.VMEM((2, NZ, NX, CH, WL), bf),
            pltpu.VMEM((TOK, WL), bf),
            pltpu.VMEM((HALF, WC), bf),
            pltpu.VMEM((HALF, WC), bf),
            pltpu.VMEM((WC, NY * WC), bf),
            pltpu.VMEM((2, HALF, WL), bf),
            pltpu.VMEM((2, HALF, WL), bf),
            pltpu.VMEM((2, 2, HALF, WL), bf),
            pltpu.VMEM((2, 2, HALF, WL), bf),
            pltpu.VMEM((HALF, WL), bf),
            dma((3,)),
            dma((4,)), dma((4,)),
            dma((NF,)), dma((NF,)),
            dma((NF,)), dma((NF,)),
            dma((NF,)), dma,
            dma((NZ,)), dma((NZ,)),
            dma((NX,)), dma((NX,)),
            dma((6,)), dma((6,)),
        ],
        compiler_params=pltpu.CompilerParams(
            collective_id=slots, has_side_effects=True, vmem_limit_bytes=56 * 1024 * 1024
        ),
    )(kinds, qkv, weight)


def local(qkv, head_kinds, out_weight):
    return attention(HC, head_kinds, qkv.transpose(1, 0, 2), out_weight)


def solution(mesh):
    placed = (P("frame", None, "head"), P(), P("head", None))
    return jax.shard_map(
        local, mesh=mesh, in_specs=placed, out_specs=P("frame", "head"), check_vma=False
    )
```

time: 313 us -> 184 us (0.59)
  waiting for transfers between devices: 198 us -> 0 us
  Pallas kernels: 0 us -> 179 us
  local copies, waits for them, and re-layouts: 41 us -> 2.09 us
  matrix products: 24.4 us -> 0 us
  starting transfers between devices: 20.3 us -> 0 us
  between operations: 15.4 us -> 0.01 us
  other arithmetic: 13 us -> 0 us
    pallas_call x0 -> x1, Pallas kernels: none -> 179 us  [attention(): pl.pallas_call(functools.partial(kernel, slots), out_shape=jax.ShapeDtype...]
    all_to_all x2 -> x0, waiting for transfers between devices: 77.2 us -> none  [the longest x1 77.2 us: local(): lax.all_to_all(arranged, 'frame', split_axis=1, concat_axis=0, tiled=True)]
    psum x1 -> x0, waiting for transfers between devices: 75.2 us -> none  [broadcast(): return lax.psum(jnp.where(mine, array, jnp.zeros_like(array)), axis)]
    unnamed x3 -> x0, waiting for transfers between devices: 45.7 us -> none
    dot_general x15 -> x0, matrix products: 24.4 us -> none  [the longest x6 9.39 us: attend(): jnp.dot(queries, key_rows.T, preferred_element_type=jnp.float32) * scale]
    all_to_all x2 -> x0, starting transfers between devices: 20.2 us -> none  [the longest x1 12.1 us: local(): lax.all_to_all(arranged, 'frame', split_axis=1, concat_axis=0, tiled=True)]
    unnamed x11 -> x1, local copies, waits for them, and re-layouts: 15.4 us -> 2.09 us
    reshape x2 -> x0, local copies, waits for them, and re-layouts: 7.41 us -> none  [the longest x1 5.76 us: local(): arranged = qkv.reshape(1, tok_rows, 3, heads_here, HD)]
  transfers between devices with their start and end apart: 4 -> 0, of which waited for: 3 -> 0; matrix products, arithmetic and copies ran while one was open for 6% -> 0% of each run, Pallas kernels for 0% -> 0%
where the time goes in v1:
time: 184 us; the launch traced here: 181 us
  Pallas kernels  179 us (97%)
  local copies, waits for them, and re-layouts  2.09 us (1%)
    pallas_call x1, Pallas kernels, attention(): pl.pallas_call(functools.partial(kernel, slots), out_shape=jax.ShapeDtype...  179 us

profile of v1, /device:TPU:1, one launch (start us, length us, event | category | flops | bytes accessed | tf_op | source)
XLA Modules:
  0.0 180.7 jit_solution(16534674490574440932)
XLA Ops:
  0.0 178.6 %shard_map.37 = bf16[1024,384]{1,0:T(8,128)(2,1)} custom-call(s32[24]{0:T(128)} %kinds.1, bf16[3,1024,384]{2,1,0:T(8,128)(2,1)} %bitcast.1, bf16[384,3072]{1,0:T(8,128)(2,1)} %weight.1), custom_call_target="tpu_custom_call" | custom-call | tf_op jit(solution)/shard_map/pallas_call | solution.py:352
  178.6 2.1 %copy.5 = bf16[1024,384]{1,0:T(8,128)(2,1)} copy(bf16[1024,384]{1,0:T(8,128)(2,1)} %shard_map.37) | data formatting | bytes 1572864

commit v2 on v1

v2 whole, which is shorter than its diff:
```python
import functools

import jax
import jax.numpy as jnp
from jax import lax
from jax.experimental import pallas as pl
from jax.experimental.pallas import tpu as pltpu
from jax.sharding import PartitionSpec as P

HD = 128
MESH = pl.DeviceIdType.MESH
NX = 4
NZ = 8
NF = NX * NZ
NY = 4
HL = 3
HC = 2 * HL
TOK = 1024
HALF = TOK // 2
ROWS = HALF // NF
CH = TOK // NF
WL = HL * HD
WC = HC * HD
QB = 256
PB = 128
SLOTS = (3, 4, 5, 6)
GAIN = HD ** -0.5 * 1.4426950408889634


def rdma(src, dst, send_sem, recv_sem, where):
    return pltpu.make_async_remote_copy(
        src_ref=src, dst_ref=dst, send_sem=send_sem, recv_sem=recv_sem,
        device_id=where, device_id_type=MESH,
    )


def dot_t(a, b):
    return lax.dot_general(a, b, (((1,), (1,)), ((), ())), preferred_element_type=jnp.float32)


def dot(a, b):
    return jnp.dot(a, b, preferred_element_type=jnp.float32)


def kernel(
    slots, kinds, qkv_in, weight, out,
    qkv, run_max, run_norm, run_mix, qkv6, stage, recv, ostage, oret, kv0, satt, att6, att, wfull,
    far_out, far_in, near_out, near_in, swap_out,
    loc_sem, px_send, px_recv, a_send, a_recv, o_send, o_recv,
    sc_send, sc_recv, zu_send, zd_send, z_recv, x_send, x_recv, y_send, y_recv,
):
    me = lax.axis_index("frame")
    mh = lax.axis_index("head")
    z, x = me // NX, me % NX
    y, c = mh // 2, mh % 2
    other = 1 - c
    partner = {"head": y * 2 + other}
    plus = {"head": lax.rem(y + 1, NY) * 2 + c}
    minus = {"head": lax.rem(y + NY - 1, NY) * 2 + c}

    barrier = pltpu.get_barrier_semaphore()

    def greet(j, carry):
        pl.semaphore_signal(
            barrier, inc=1, device_id={"frame": lax.rem(me + j, NF)}, device_id_type=MESH
        )
        return carry

    lax.fori_loop(1, NF, greet, 0)
    for who in (partner, plus, minus):
        pl.semaphore_signal(barrier, inc=1, device_id=who, device_id_type=MESH)

    my_rows = pl.ds(pl.multiple_of(c * HALF, HALF), HALF)
    other_rows = pl.ds(pl.multiple_of(other * HALF, HALF), HALF)
    my_lanes = pl.ds(pl.multiple_of(c * WL, HD), WL)
    other_lanes = pl.ds(pl.multiple_of(other * WL, HD), WL)
    my_wrows = pl.ds(pl.multiple_of(c * WL, HD), WL)

    load = pltpu.make_async_copy(qkv_in, qkv, loc_sem.at[3])
    load.start()
    own_qkv = pltpu.make_async_copy(
        qkv_in.at[:, my_rows, :], qkv6.at[:, :, my_lanes], loc_sem.at[0]
    )
    own_qkv.start()
    own_w = pltpu.make_async_copy(weight, wfull.at[my_wrows, :], loc_sem.at[1])
    own_w.start()

    load.wait()

    def own_frame(n, carry):
        h = n // (TOK // QB)
        rows = pl.ds(pl.multiple_of(n % (TOK // QB) * QB, QB), QB)
        lanes = pl.ds(pl.multiple_of(h * HD, HD), HD)
        s = dot_t(qkv[0, rows, lanes], qkv[1, :, lanes])
        top = jnp.max(s, axis=-1, keepdims=True)
        e = jnp.exp2((s - top) * GAIN)
        run_max[h, rows] = top
        run_norm[h, rows] = jnp.sum(e, axis=-1, keepdims=True)
        run_mix[rows, lanes] = dot(e.astype(jnp.bfloat16), qkv[2, :, lanes])
        return carry

    lax.fori_loop(0, HL * (TOK // QB), own_frame, 0)

    pl.semaphore_wait(barrier, NF - 1 + 3)

    swap = rdma(
        qkv_in.at[:, other_rows, :], qkv6.at[:, :, my_lanes], px_send.at[0], px_recv.at[0], partner
    )
    swap.start()

    @pl.when(me == 0)
    def _():
        own_chunk = pltpu.make_async_copy(
            qkv_in.at[pl.ds(1, 2), pl.ds(0, CH), :], kv0.at[:, 0, 0], sc_recv
        )
        own_chunk.start()

        def scatter(j, carry):
            rows = pl.ds(pl.multiple_of(j * CH, CH), CH)
            rdma(
                qkv_in.at[pl.ds(1, 2), rows, :], kv0.at[:, j // NX, j % NX],
                sc_send.at[j], sc_recv, {"frame": j},
            ).start()
            return carry

        lax.fori_loop(1, NF, scatter, 0)

    own_qkv.wait()
    rdma(
        qkv.at[:, my_rows, :], qkv6.at[:, :, other_lanes], px_send.at[0], px_recv.at[0], partner
    ).wait_recv()

    kind = [kinds[y * HC + h] for h in range(HC)]
    place = [0]
    for h in range(HC - 1):
        place.append(place[-1] + kind[h])
    for t in range(slots):
        for i in range(3):
            part = qkv6[i, :, t * HD : (t + 1) * HD]
            if slots < HC:
                for h in range(t + 1, HC):
                    here = (kind[h] == 1) & (place[h] == t)
                    part = jnp.where(here, qkv6[i, :, h * HD : (h + 1) * HD], part)
            stage[:, t, i] = part.reshape(NF, ROWS, HD)

    pltpu.make_async_copy(
        qkv.at[pl.ds(1, 2), pl.ds(0, CH), :], kv0.at[:, z, x], sc_recv
    ).wait()

    z_up = {"frame": lax.rem(z + 1, NZ) * NX + x}
    z_down = {"frame": lax.rem(z + NZ - 1, NZ) * NX + x}
    x_up = {"frame": z * NX + lax.rem(x + 1, NX)}
    x_down = {"frame": z * NX + lax.rem(x + NX - 1, NX)}
    x_far = {"frame": z * NX + lax.rem(x + 2, NX)}
    ring = []

    def pass_on(src, send_sem, recv_sem, who):
        copy = rdma(src, src, send_sem, recv_sem, who)
        copy.start()
        ring.append(copy)

    def arrived(part, recv_sem):
        rdma(part, part, zu_send.at[0, 0], recv_sem, z_up).wait_recv()

    def z_part(at, h):
        return kv0.at[:, at, x, :, h * HD : (h + 1) * HD]

    def x_part(at, h):
        return kv0.at[:, :, at, :, h * HD : (h + 1) * HD]

    for step in range(NZ // 2):
        low = lax.rem(z + NZ - step, NZ)
        high = lax.rem(z + step, NZ)
        for h in range(HL):
            if step > 0:
                arrived(z_part(low, h), z_recv.at[h, low])
            pass_on(z_part(low, h), zu_send.at[h, step], z_recv.at[h, low], z_up)
            if step < NZ // 2 - 1:
                if step > 0:
                    arrived(z_part(high, h), z_recv.at[h, high])
                pass_on(z_part(high, h), zd_send.at[h, step], z_recv.at[h, high], z_down)
    for h in range(HL):
        for at in (lax.rem(z + NZ // 2, NZ), lax.rem(z + NZ // 2 - 1, NZ)):
            arrived(z_part(at, h), z_recv.at[h, at])
        for j, who in enumerate((x_far, x_up, x_down)):
            pass_on(x_part(x, h), x_send.at[h, j], x_recv.at[h, x], who)

    def send_parts(j, carry):
        to = lax.rem(me + j, NF)
        rdma(stage.at[to], recv.at[me], a_send.at[to], a_recv.at[me], {"frame": to}).start()
        return carry

    lax.fori_loop(1, NF, send_parts, 0)
    recv[pl.ds(me, 1)] = stage[pl.ds(me, 1)]

    swap_w = rdma(weight, wfull.at[my_wrows, :], px_send.at[1], px_recv.at[1], partner)
    swap_w.start()


    def wait_parts(j, carry):
        at = lax.rem(me + NF - j, NF)
        rdma(stage.at[at], recv.at[at], a_send.at[at], a_recv.at[at], {"frame": at}).wait_recv()
        return carry

    lax.fori_loop(1, NF, wait_parts, 0)

    span = NF * ROWS
    same = (
        lax.broadcasted_iota(jnp.int32, (span, span), 0) % ROWS
        == lax.broadcasted_iota(jnp.int32, (span, span), 1) % ROWS
    )

    def temporal(t, carry):
        q = recv[:, t, 0].reshape(span, HD)
        k = recv[:, t, 1].reshape(span, HD)
        v = recv[:, t, 2].reshape(span, HD)
        s = jnp.where(same, dot_t(q, k), -1e30)
        e = jnp.exp2((s - jnp.max(s, axis=-1, keepdims=True)) * GAIN)
        norm = jnp.sum(e, axis=-1, keepdims=True)
        o = dot(e.astype(jnp.bfloat16), v) / norm
        ostage[:, t] = o.astype(jnp.bfloat16).reshape(NF, ROWS, HD)
        return carry

    lax.fori_loop(0, slots, temporal, 0)

    def send_back(j, carry):
        to = lax.rem(me + j, NF)
        rdma(ostage.at[to], oret.at[me], o_send.at[to], o_recv.at[me], {"frame": to}).start()
        return carry

    lax.fori_loop(1, NF, send_back, 0)
    oret[pl.ds(me, 1)] = ostage[pl.ds(me, 1)]


    def wait_x(n, carry):
        h, j = n // (NX - 1), n % (NX - 1) + 1
        at = lax.rem(x + j, NX)
        part = kv0.at[:, :, at, :, pl.ds(pl.multiple_of(h * HD, HD), HD)]
        arrived(part, x_recv.at[h, at])
        return carry

    lax.fori_loop(0, HL * (NX - 1), wait_x, 0)

    def first_frame(n, carry):
        h = n // (TOK // QB)
        rows = pl.ds(pl.multiple_of(n % (TOK // QB) * QB, QB), QB)
        lanes = pl.ds(pl.multiple_of(h * HD, HD), HD)
        s = dot_t(qkv[0, rows, lanes], kv0[0, :, :, :, lanes].reshape(TOK, HD))
        s = jnp.where(me == 0, -1e30, s)
        before = run_max[h, rows]
        top = jnp.maximum(before, jnp.max(s, axis=-1, keepdims=True))
        keep = jnp.exp2((before - top) * GAIN)
        e = jnp.exp2((s - top) * GAIN)
        norm = run_norm[h, rows] * keep + jnp.sum(e, axis=-1, keepdims=True)
        mixed = run_mix[rows, lanes] * keep + dot(
            e.astype(jnp.bfloat16), kv0[1, :, :, :, lanes].reshape(TOK, HD)
        )
        satt[rows, lanes] = (mixed / norm).astype(jnp.bfloat16)
        return carry

    lax.fori_loop(0, HL * (TOK // QB), first_frame, 0)

    swap_s = rdma(
        satt.at[other_rows, :], att6.at[:, my_lanes], px_send.at[2], px_recv.at[2], partner
    )
    swap_s.start()
    own_s = pltpu.make_async_copy(satt.at[my_rows, :], att6.at[:, my_lanes], loc_sem.at[2])
    own_s.start()

    own_s.wait()
    rdma(
        satt.at[my_rows, :], att6.at[:, other_lanes], px_send.at[2], px_recv.at[2], partner
    ).wait_recv()
    own_w.wait()
    rdma(
        weight, wfull.at[pl.ds(pl.multiple_of(other * WL, HD), WL), :],
        px_send.at[1], px_recv.at[1], partner,
    ).wait_recv()

    def wait_back(j, carry):
        at = lax.rem(me + NF - j, NF)
        rdma(ostage.at[at], oret.at[at], o_send.at[at], o_recv.at[at], {"frame": at}).wait_recv()
        return carry

    lax.fori_loop(1, NF, wait_back, 0)

    for h in range(HC):
        lanes = slice(h * HD, (h + 1) * HD)
        part = att6[:, lanes]
        for t in range(min(h + 1, slots)) if slots < HC else [h]:
            here = (kind[h] == 1) & (place[h] == t) if slots < HC else kind[h] == 1
            part = jnp.where(here, oret[:, t].reshape(HALF, HD), part)
        att[:, lanes] = part

    def product(dst, block, half, *more):
        lanes = pl.ds(pl.multiple_of(block * WC + half * WL, HD), WL)

        def piece(b, carry):
            rows = pl.ds(pl.multiple_of(b * PB, PB), PB)
            total = dot(att[rows, :], wfull[:, lanes])
            for extra in more:
                total += extra[rows, :].astype(jnp.float32)
            dst[rows, :] = total.astype(jnp.bfloat16)
            return carry

        lax.fori_loop(0, HALF // PB, piece, 0)

    up, down, far = lax.rem(y + 1, NY), lax.rem(y + NY - 1, NY), lax.rem(y + 2, NY)
    sends = []

    def send(src, dst, index, who):
        copy = rdma(src, dst, y_send.at[index], y_recv.at[index], who)
        copy.start()
        sends.append(copy)

    product(far_out.at[0], far, 0)
    send(far_out.at[0], far_in.at[0], 0, plus)
    product(far_out.at[1], far, 1)
    send(far_out.at[1], far_in.at[1], 1, minus)
    product(near_out.at[0, 1], up, 1)
    send(near_out.at[0, 1], near_in.at[0, 1], 2, plus)
    product(near_out.at[1, 0], down, 0)
    send(near_out.at[1, 0], near_in.at[1, 0], 3, minus)
    sends[0].wait_recv()
    product(near_out.at[0, 0], up, 0, far_in.at[0])
    send(near_out.at[0, 0], near_in.at[0, 0], 4, plus)
    sends[1].wait_recv()
    product(near_out.at[1, 1], down, 1, far_in.at[1])
    send(near_out.at[1, 1], near_in.at[1, 1], 5, minus)

    for index in range(2, 6):
        sends[index].wait_recv()

    product(swap_out, y, other, near_in.at[0, other], near_in.at[1, other])
    last = rdma(swap_out, out.at[my_rows, :], px_send.at[3], px_recv.at[3], partner)
    last.start()
    product(out.at[my_rows, :], y, c, near_in.at[0, c], near_in.at[1, c])
    rdma(swap_out, out.at[other_rows, :], px_send.at[3], px_recv.at[3], partner).wait_recv()

    swap.wait_send()
    swap_w.wait_send()
    swap_s.wait_send()
    last.wait_send()
    for copy in sends:
        copy.wait_send()

    def drain(j, carry):
        to = lax.rem(me + j, NF)
        rdma(stage.at[to], recv.at[me], a_send.at[to], a_recv.at[me], {"frame": to}).wait_send()
        rdma(ostage.at[to], oret.at[me], o_send.at[to], o_recv.at[me], {"frame": to}).wait_send()
        return carry

    lax.fori_loop(1, NF, drain, 0)

    for copy in ring:
        copy.wait_send()

    @pl.when(me == 0)
    def _():
        def drain_s(j, carry):
            rows = pl.ds(pl.multiple_of(j * CH, CH), CH)
            rdma(
                qkv_in.at[pl.ds(1, 2), rows, :], kv0.at[:, j // NX, j % NX],
                sc_send.at[j], sc_recv, {"frame": j},
            ).wait_send()
            return carry

        lax.fori_loop(1, NF, drain_s, 0)


def attention(slots, kinds, qkv, weight):
    bf = jnp.bfloat16
    vmem = pl.BlockSpec(memory_space=pltpu.VMEM)
    hbm = pl.BlockSpec(memory_space=pl.ANY)
    dma = pltpu.SemaphoreType.DMA
    return pl.pallas_call(
        functools.partial(kernel, slots),
        out_shape=jax.ShapeDtypeStruct((TOK, WL), bf),
        in_specs=[pl.BlockSpec(memory_space=pltpu.SMEM), hbm, hbm],
        out_specs=vmem,
        scratch_shapes=[
            pltpu.VMEM((3, TOK, WL), bf),
            pltpu.VMEM((HL, TOK, 1), jnp.float32),
            pltpu.VMEM((HL, TOK, 1), jnp.float32),
            pltpu.VMEM((TOK, WL), jnp.float32),
            pltpu.VMEM((3, HALF, WC), bf),
            pltpu.VMEM((NF, slots, 3, ROWS, HD), bf),
            pltpu.VMEM((NF, slots, 3, ROWS, HD), bf),
            pltpu.VMEM((NF, slots, ROWS, HD), bf),
            pltpu.VMEM((NF, slots, ROWS, HD), bf),
            pltpu.VMEM((2, NZ, NX, CH, WL), bf),
            pltpu.VMEM((TOK, WL), bf),
            pltpu.VMEM((HALF, WC), bf),
            pltpu.VMEM((HALF, WC), bf),
            pltpu.VMEM((WC, NY * WC), bf),
            pltpu.VMEM((2, HALF, WL), bf),
            pltpu.VMEM((2, HALF, WL), bf),
            pltpu.VMEM((2, 2, HALF, WL), bf),
            pltpu.VMEM((2, 2, HALF, WL), bf),
            pltpu.VMEM((HALF, WL), bf),
            dma((4,)),
            dma((4,)), dma((4,)),
            dma((NF,)), dma((NF,)),
            dma((NF,)), dma((NF,)),
            dma((NF,)), dma,
            dma((HL, NZ)), dma((HL, NZ)), dma((HL, NZ)),
            dma((HL, NX)), dma((HL, NX)),
            dma((6,)), dma((6,)),
        ],
        compiler_params=pltpu.CompilerParams(
            collective_id=slots, has_side_effects=True, vmem_limit_bytes=56 * 1024 * 1024
        ),
    )(kinds, qkv, weight)


def local(qkv, head_kinds, out_weight):
    most = jnp.max(jnp.sum(
        jnp.where(jnp.arange(NY * HC) // HC == jnp.arange(NY)[:, None], head_kinds, 0), axis=1
    ))
    choices = [functools.partial(attention, slots) for slots in SLOTS]
    return lax.switch(
        jnp.clip(most - SLOTS[0], 0, len(SLOTS) - 1),
        choices, head_kinds, qkv.transpose(1, 0, 2), out_weight,
    )


def solution(mesh):
    placed = (P("frame", None, "head"), P(), P("head", None))
    return jax.shard_map(
        local, mesh=mesh, in_specs=placed, out_specs=P("frame", "head"), check_vma=False
    )
```

time: 184 us -> 145 us (0.79); the launches traced: 181 us -> 145 us
  Pallas kernels: 179 us -> 141 us
    pallas_call x1, Pallas kernels: 179 us -> 141 us  [attention(): pl.pallas_call(functools.partial(kernel, slots), out_shape=jax.ShapeDtype...]
where the time goes in v2:
time: 145 us
  Pallas kernels  141 us (97%)
    pallas_call x1, Pallas kernels, attention(): pl.pallas_call(functools.partial(kernel, slots), out_shape=jax.ShapeDtype...  141 us

profile of v2, /device:TPU:1, one launch (start us, length us, event | category | flops | bytes accessed | tf_op | source)
XLA Modules:
  0.0 144.6 jit_solution(10285221075475505384)
XLA Ops:
  0.0 0.8 select_reduce_fusion
  0.8 0.6 reduce_max.9
  2.1 141.6 %conditional.1 = (bf16[1024,384]{1,0:T(8,128)(2,1)S(1)}) conditional(s32[]{:T(128)} %clamp.3, (s32[24]{0:T(128)}, bf16[3,1024,384]{2,1,0:T(8,128)(2,1)}, bf16[384,3072]{1,0:T(8,128)(2,1)}) %tuple.26, (s32[24]{0:T(128)}, bf16[3,1024,384]{2,1,0:T(8,128)(2,1)}, bf16[384,3072]{1,0:T(8,128)(2,1)}) %tuple.27, ...), branch_computations={%region_2.3_spmd, %region_3.4_spmd, %region_4.5_spmd, %region_5.6_... | conditional | bytes 8 | solution.py:421
  2.3 141.4 %branch_2_fun.1 = bf16[1024,384]{1,0:T(8,128)(2,1)S(1)} custom-call(s32[24]{0:T(128)} %get-tuple-element.40.kinds, bf16[3,1024,384]{2,1,0:T(8,128)(2,1)} %get-tuple-element.41.qkv_in, bf16[384,3072]{1,0:T(8,128)(2,1)} %get-tuple-element.53.weight), custom_call_target="tpu_custom_call" | custom-call | tf_op jit(solution)/shard_map/cond/branch_2_fun/pallas_call | solution.py:376
  143.7 0.9 copy.17
  (1 shorter events, 0.0 us)

commit v3 on v2

v3 whole, which is shorter than its diff:
```python
import functools

import jax
import jax.numpy as jnp
from jax import lax
from jax.experimental import pallas as pl
from jax.experimental.pallas import tpu as pltpu
from jax.sharding import PartitionSpec as P

HD = 128
MESH = pl.DeviceIdType.MESH
NX = 4
NZ = 8
NF = NX * NZ
NY = 4
HL = 3
HC = 2 * HL
TOK = 1024
HALF = TOK // 2
ROWS = HALF // NF
PART = ROWS // 2
CH = TOK // NF
WL = HL * HD
WC = HC * HD
QB = 256
PB = 128
NP = PB // ROWS
SIZES = ((4, 4), (4, 5), (5, 4), (5, 5), (HC, HC))
GAIN = HD ** -0.5 * 1.4426950408889634


def rdma(src, dst, send_sem, recv_sem, where):
    return pltpu.make_async_remote_copy(
        src_ref=src, dst_ref=dst, send_sem=send_sem, recv_sem=recv_sem,
        device_id=where, device_id_type=MESH,
    )


def dot_t(a, b):
    return lax.dot_general(a, b, (((1,), (1,)), ((), ())), preferred_element_type=jnp.float32)


def dot(a, b):
    return jnp.dot(a, b, preferred_element_type=jnp.float32)


def kernel(
    slots, frees, kinds, qkv_in, weight, out,
    qkv6, kv_other, stage, recv, ostage, oret, kvst, kv0, kv1, sel, satt, att6, att, wfull,
    far_out, far_in, near_out, near_in, swap_out, swap_in, mine,
    loc_sem, px_send, px_recv, a_send, a_recv, o_send, o_recv,
    sc_send, sc_recv, zu_send, zd_send, z_recv, x_send, x_recv, y_send, y_recv,
):
    me = lax.axis_index("frame")
    mh = lax.axis_index("head")
    z, x = me // NX, me % NX
    y, c = mh // 2, mh % 2
    other = 1 - c
    partner = {"head": y * 2 + other}
    plus = {"head": lax.rem(y + 1, NY) * 2 + c}
    minus = {"head": lax.rem(y + NY - 1, NY) * 2 + c}

    barrier = pltpu.get_barrier_semaphore()

    def greet(j, carry):
        pl.semaphore_signal(
            barrier, inc=1, device_id={"frame": lax.rem(me + j, NF)}, device_id_type=MESH
        )
        return carry

    lax.fori_loop(1, NF, greet, 0)
    for who in (partner, plus, minus):
        pl.semaphore_signal(barrier, inc=1, device_id=who, device_id_type=MESH)

    my_rows = pl.ds(pl.multiple_of(c * HALF, HALF), HALF)
    other_rows = pl.ds(pl.multiple_of(other * HALF, HALF), HALF)
    my_lanes = pl.ds(pl.multiple_of(c * WL, HD), WL)
    other_lanes = pl.ds(pl.multiple_of(other * WL, HD), WL)
    my_wrows = pl.ds(pl.multiple_of(c * WL, HD), WL)

    own_qkv = pltpu.make_async_copy(
        qkv_in.at[:, my_rows, :], qkv6.at[:, :, my_lanes], loc_sem.at[0]
    )
    own_qkv.start()
    own_w = pltpu.make_async_copy(weight, wfull.at[my_wrows, :], loc_sem.at[1])
    own_w.start()

    own_kv = pltpu.make_async_copy(
        qkv_in.at[pl.ds(1, 2), other_rows, :], kv_other.at[:, :, my_lanes], loc_sem.at[2]
    )
    own_kv.start()

    pl.semaphore_wait(barrier, NF - 1 + 3)

    swap = rdma(
        qkv_in.at[:, other_rows, :], qkv6.at[:, :, my_lanes], px_send.at[0], px_recv.at[0], partner
    )
    swap.start()

    own_qkv.wait()
    rdma(
        qkv_in.at[:, my_rows, :], qkv6.at[:, :, other_lanes], px_send.at[0], px_recv.at[0], partner
    ).wait_recv()

    kind = [kinds[y * HC + h] for h in range(HC)]
    place = [0]
    for h in range(HC - 1):
        place.append(place[-1] + kind[h])
    free = [h - place[h] for h in range(HC)]

    def chosen(ref, i, rows, wanted, place_of, slot, low):
        part = ref[i, rows, low * HD : (low + 1) * HD]
        for h in range(low + 1, HC):
            here = (kind[h] == wanted) & (place_of[h] == slot)
            part = jnp.where(here, ref[i, rows, h * HD : (h + 1) * HD], part)
        return part

    def in_pieces(body):
        def step(b, carry):
            body(b, pl.ds(pl.multiple_of(b * PB, PB), PB))
            return carry

        lax.fori_loop(0, HALF // PB, step, 0)

    @pl.when(me == 0)
    def _():
        def fill_first(b, rows):
            for n in range(frees):
                for i in range(2):
                    part = chosen(qkv6, 1 + i, rows, 0, free, n, n)
                    kvst[pl.ds(b * NP, NP), n, i] = part.reshape(NP, ROWS, HD)

        in_pieces(fill_first)
        pltpu.make_async_copy(kvst.at[0], kv0.at[0, 0], sc_recv).start()

        def scatter(j, carry):
            rdma(
                kvst.at[j], kv0.at[j // NX, j % NX], sc_send.at[j], sc_recv, {"frame": j}
            ).start()
            return carry

        lax.fori_loop(1, NF, scatter, 0)

    def fill_stage(b, rows):
        for t in range(slots):
            for i in range(3):
                part = chosen(qkv6, i, rows, 1, place, t, t)
                stage[pl.ds(b * NP, NP), t, i] = part.reshape(NP, ROWS, HD)

    in_pieces(fill_stage)

    def send_part(dz, dx):
        to = lax.rem(z + dz, NZ) * NX + lax.rem(x + dx, NX)
        rdma(stage.at[to], recv.at[me], a_send.at[to], a_recv.at[me], {"frame": to}).start()

    def turn(n):
        odd = lax.rem(n, 2)
        return odd * ((n + 1) // 2) + (1 - odd) * (NZ - n // 2)

    def send_straight(n, carry):
        send_part(turn(n), 0)
        return carry

    def send_row(n, carry):
        send_part(0, n)
        return carry

    def send_rest(n, carry):
        send_part(turn(n // (NX - 1) + 1), n % (NX - 1) + 1)
        return carry

    pltpu.make_async_copy(kvst.at[0], kv0.at[z, x], sc_recv).wait()

    z_up = {"frame": lax.rem(z + 1, NZ) * NX + x}
    z_down = {"frame": lax.rem(z + NZ - 1, NZ) * NX + x}
    x_up = {"frame": z * NX + lax.rem(x + 1, NX)}
    x_down = {"frame": z * NX + lax.rem(x + NX - 1, NX)}
    ring = []

    def pass_on(src, send_sem, recv_sem, who):
        copy = rdma(src, src, send_sem, recv_sem, who)
        copy.start()
        ring.append(copy)

    def arrived(part, recv_sem):
        rdma(part, part, zu_send.at[0], recv_sem, z_up).wait_recv()

    for step in range(NZ // 2):
        low = lax.rem(z + NZ - step, NZ)
        high = lax.rem(z + step, NZ)
        if step > 0:
            arrived(kv0.at[low, x], z_recv.at[low])
        pass_on(kv0.at[low, x], zu_send.at[step], z_recv.at[low], z_up)
        if step < NZ // 2 - 1:
            if step > 0:
                arrived(kv0.at[high, x], z_recv.at[high])
            pass_on(kv0.at[high, x], zd_send.at[step], z_recv.at[high], z_down)
    for at in (lax.rem(z + NZ // 2, NZ), lax.rem(z + NZ // 2 - 1, NZ)):
        arrived(kv0.at[at, x], z_recv.at[at])
    x_low, x_high = lax.rem(x + NX - 1, NX), lax.rem(x + 1, NX)
    x_over = lax.rem(x + 2, NX)
    pass_on(kv0.at[:, x], x_send.at[0], x_recv.at[x], x_up)
    pass_on(kv0.at[:, x], x_send.at[1], x_recv.at[x], x_down)

    lax.fori_loop(1, NZ, send_straight, 0)

    near_z, far_z = pl.ds(0, NZ // 2), pl.ds(NZ // 2, NZ // 2)
    arrived(kv0.at[:, x_low], x_recv.at[x_low])
    pass_on(kv0.at[near_z, x_low], x_send.at[2], x_recv.at[NX], x_up)
    arrived(kv0.at[:, x_high], x_recv.at[x_high])
    pass_on(kv0.at[far_z, x_high], x_send.at[3], x_recv.at[NX + 1], x_down)
    arrived(kv0.at[near_z, x_over], x_recv.at[NX])
    arrived(kv0.at[far_z, x_over], x_recv.at[NX + 1])
    share_first = rdma(kv0, kv1, px_send.at[2], px_recv.at[2], partner)
    share_first.start()
    share_kv = rdma(
        qkv_in.at[pl.ds(1, 2), my_rows, :], kv_other.at[:, :, my_lanes],
        px_send.at[5], px_recv.at[5], partner,
    )
    share_kv.start()
    lax.fori_loop(1, NX, send_row, 0)
    lax.fori_loop(0, (NZ - 1) * (NX - 1), send_rest, 0)
    recv[pl.ds(me, 1)] = stage[pl.ds(me, 1)]

    swap_w = rdma(weight, wfull.at[my_wrows, :], px_send.at[1], px_recv.at[1], partner)
    swap_w.start()


    own_kv.wait()
    share_first.wait_recv()
    rdma(
        qkv_in.at[pl.ds(1, 2), my_rows, :], kv_other.at[:, :, other_lanes],
        px_send.at[5], px_recv.at[5], partner,
    ).wait_recv()

    def spatial(n, carry):
        def select(b, rows):
            for at, (ref, i) in enumerate(
                ((qkv6, 0), (qkv6, 1), (kv_other, 0), (qkv6, 2), (kv_other, 1))
            ):
                sel[at, rows, :] = chosen(ref, i, rows, 0, free, n, 0)

        in_pieces(select)

        def block(b, inner):
            rows = pl.ds(pl.multiple_of(b * QB, QB), QB)
            q = sel[0, rows, :]
            firsts = [ref[:, :, n, 0].reshape(HALF, HD) for ref in (kv0, kv1)]
            scores = [dot_t(q, sel[1]), dot_t(q, sel[2])]
            scores += [jnp.where(me == 0, -1e30, dot_t(q, keys)) for keys in firsts]
            top = functools.reduce(
                jnp.maximum, [jnp.max(s, axis=-1, keepdims=True) for s in scores]
            )
            values = [sel[3], sel[4]] + [ref[:, :, n, 1].reshape(HALF, HD) for ref in (kv0, kv1)]
            norm, mixed = 0.0, 0.0
            for s, v in zip(scores, values):
                e = jnp.exp2((s - top) * GAIN)
                norm += jnp.sum(e, axis=-1, keepdims=True)
                mixed += dot(e.astype(jnp.bfloat16), v)
            satt[n, rows, :] = (mixed / norm).astype(jnp.bfloat16)
            return inner

        return lax.fori_loop(0, HALF // QB, block, carry)

    lax.fori_loop(0, frees, spatial, 0)

    def rows_of(tile, k):
        wide = tile.astype(jnp.float32)
        return wide[:, k * PART : (k + 1) * PART].reshape(-1, HD)

    def order(b, rows):
        for h in range(HC):
            part = satt[0, rows, :]
            for n in range(1, min(h + 1, frees)):
                part = jnp.where(free[h] == n, satt[n, rows, :], part)
            for k in range(2):
                att6[k, pl.ds(pl.multiple_of(b * PB // 2, PB // 2), PB // 2), h * HD : (h + 1) * HD] = (
                    rows_of(part.reshape(NP, ROWS, HD), k).astype(jnp.bfloat16)
                )

    in_pieces(order)
    own_w.wait()
    rdma(
        weight, wfull.at[pl.ds(pl.multiple_of(other * WL, HD), WL), :],
        px_send.at[1], px_recv.at[1], partner,
    ).wait_recv()

    def wait_parts(j, carry):
        at = lax.rem(me + NF - j, NF)
        rdma(stage.at[at], recv.at[at], a_send.at[at], a_recv.at[at], {"frame": at}).wait_recv()
        return carry

    lax.fori_loop(1, NF, wait_parts, 0)

    span = NF * PART
    same = (
        lax.broadcasted_iota(jnp.int32, (span, span), 0) % PART
        == lax.broadcasted_iota(jnp.int32, (span, span), 1) % PART
    )

    def temporal(t, k):
        q, key, v = (rows_of(recv[:, t, i], k).astype(jnp.bfloat16) for i in range(3))
        s = jnp.where(same, dot_t(q, key), -1e30)
        e = jnp.exp2((s - jnp.max(s, axis=-1, keepdims=True)) * GAIN)
        norm = jnp.sum(e, axis=-1, keepdims=True)
        return (dot(e.astype(jnp.bfloat16), v) / norm).reshape(NF, PART, HD)

    def back(to, k):
        return rdma(
            ostage.at[to, k], oret.at[me, k], o_send.at[k, to], o_recv.at[k, me], {"frame": to}
        )

    for k in range(2):

        def pair(n, carry, k=k):
            both = [temporal(jnp.minimum(2 * n + i, slots - 1), k) for i in range(2)]
            ostage[:, k, n] = jnp.concatenate(both, axis=1).astype(jnp.bfloat16)
            return carry

        lax.fori_loop(0, (slots + 1) // 2, pair, 0)

        def send_back(j, carry, k=k):
            back(lax.rem(me + j, NF), k).start()
            return carry

        lax.fori_loop(1, NF, send_back, 0)
        oret[pl.ds(me, 1), k] = ostage[pl.ds(me, 1), k]

    def product(dst, k, block, half, *more):
        lanes = pl.ds(pl.multiple_of(block * WC + half * WL, HD), WL)

        def piece(b, carry):
            rows = pl.ds(pl.multiple_of(b * PB, PB), PB)
            total = dot(att[k, rows, :], wfull[:, lanes])
            for extra in more:
                total += extra[rows, :].astype(jnp.float32)
            dst[rows, :] = total.astype(jnp.bfloat16)
            return carry

        lax.fori_loop(0, span // PB, piece, 0)

    up, down, far = lax.rem(y + 1, NY), lax.rem(y + NY - 1, NY), lax.rem(y + 2, NY)

    def y_copy(k, index):
        parts = (
            (far_out.at[k, 0], far_in.at[k, 0], plus),
            (far_out.at[k, 1], far_in.at[k, 1], minus),
            (near_out.at[k, 0, 1], near_in.at[k, 0, 1], plus),
            (near_out.at[k, 1, 0], near_in.at[k, 1, 0], minus),
            (near_out.at[k, 0, 0], near_in.at[k, 0, 0], plus),
            (near_out.at[k, 1, 1], near_in.at[k, 1, 1], minus),
        )
        src, dst, who = parts[index]
        return rdma(src, dst, y_send.at[k, index], y_recv.at[k, index], who)

    def reduce_chunk(k, carry):
        def wait_back(j, inner):
            at = lax.rem(me + NF - j, NF)
            rdma(
                ostage.at[at, k], oret.at[at, k], o_send.at[k, at], o_recv.at[k, at],
                {"frame": at},
            ).wait_recv()
            return inner

        lax.fori_loop(1, NF, wait_back, 0)

        def gather(b, rows):
            half_rows = pl.ds(pl.multiple_of(b * PB // 2, PB // 2), PB // 2)
            for h in range(HC):
                lanes = slice(h * HD, (h + 1) * HD)
                part = att6[k, half_rows, lanes].astype(jnp.float32)
                for t in range(min(h + 1, slots)):
                    here = (kind[h] == 1) & (place[h] == t)
                    returned = rows_of(oret[pl.ds(b * NP, NP), k, t // 2], t % 2)
                    part = jnp.where(here, returned, part)
                att[k, half_rows, lanes] = part.astype(jnp.bfloat16)

        in_pieces(gather)

        product(far_out.at[k, 0], k, far, 0)
        y_copy(k, 0).start()
        product(far_out.at[k, 1], k, far, 1)
        y_copy(k, 1).start()
        product(near_out.at[k, 0, 1], k, up, 1)
        y_copy(k, 2).start()
        product(near_out.at[k, 1, 0], k, down, 0)
        y_copy(k, 3).start()
        y_copy(k, 0).wait_recv()
        product(near_out.at[k, 0, 0], k, up, 0, far_in.at[k, 0])
        y_copy(k, 4).start()
        y_copy(k, 1).wait_recv()
        product(near_out.at[k, 1, 1], k, down, 1, far_in.at[k, 1])
        y_copy(k, 5).start()
        return carry

    lax.fori_loop(0, 2, reduce_chunk, 0)

    def swap_copy(k):
        return rdma(
            swap_out.at[k], swap_in.at[k], px_send.at[3 + k], px_recv.at[3 + k], partner
        )

    def finish(k, carry):
        for index in range(2, 6):
            y_copy(k, index).wait_recv()
        product(swap_out.at[k], k, y, other, near_in.at[k, 0, other], near_in.at[k, 1, other])
        swap_copy(k).start()
        product(mine.at[k], k, y, c, near_in.at[k, 0, c], near_in.at[k, 1, c])
        return carry

    lax.fori_loop(0, 2, finish, 0)

    def join(src):
        tiles = [src[k].astype(jnp.float32).reshape(NF, PART, WL) for k in range(2)]
        return jnp.concatenate(tiles, axis=1).reshape(HALF, WL).astype(jnp.bfloat16)

    out[my_rows, :] = join(mine)
    for k in range(2):
        swap_copy(k).wait_recv()
    out[other_rows, :] = join(swap_in)

    swap.wait_send()
    swap_w.wait_send()
    share_first.wait_send()
    share_kv.wait_send()
    for k in range(2):
        swap_copy(k).wait_send()
        for index in range(6):
            y_copy(k, index).wait_send()

    def drain(j, carry):
        to = lax.rem(me + j, NF)
        rdma(stage.at[to], recv.at[me], a_send.at[to], a_recv.at[me], {"frame": to}).wait_send()
        back(to, 0).wait_send()
        back(to, 1).wait_send()
        return carry

    lax.fori_loop(1, NF, drain, 0)

    for copy in ring:
        copy.wait_send()

    @pl.when(me == 0)
    def _():
        def drain_s(j, carry):
            rdma(
                kvst.at[j], kv0.at[j // NX, j % NX], sc_send.at[j], sc_recv, {"frame": j}
            ).wait_send()
            return carry

        lax.fori_loop(1, NF, drain_s, 0)


def attention(slots, frees, ident, kinds, qkv, weight):
    bf = jnp.bfloat16
    vmem = pl.BlockSpec(memory_space=pltpu.VMEM)
    hbm = pl.BlockSpec(memory_space=pl.ANY)
    dma = pltpu.SemaphoreType.DMA
    return pl.pallas_call(
        functools.partial(kernel, slots, frees),
        out_shape=jax.ShapeDtypeStruct((TOK, WL), bf),
        in_specs=[pl.BlockSpec(memory_space=pltpu.SMEM), hbm, hbm],
        out_specs=vmem,
        scratch_shapes=[
            pltpu.VMEM((3, HALF, WC), bf),
            pltpu.VMEM((2, HALF, WC), bf),
            pltpu.VMEM((NF, slots, 3, ROWS, HD), bf),
            pltpu.VMEM((NF, slots, 3, ROWS, HD), bf),
            pltpu.VMEM((NF, 2, (slots + 1) // 2, ROWS, HD), bf),
            pltpu.VMEM((NF, 2, (slots + 1) // 2, ROWS, HD), bf),
            pltpu.VMEM((NF, frees, 2, ROWS, HD), bf),
            pltpu.VMEM((NZ, NX, frees, 2, ROWS, HD), bf),
            pltpu.VMEM((NZ, NX, frees, 2, ROWS, HD), bf),
            pltpu.VMEM((5, HALF, HD), bf),
            pltpu.VMEM((frees, HALF, HD), bf),
            pltpu.VMEM((2, HALF // 2, WC), bf),
            pltpu.VMEM((2, HALF // 2, WC), bf),
            pltpu.VMEM((WC, NY * WC), bf),
            pltpu.VMEM((2, 2, HALF // 2, WL), bf),
            pltpu.VMEM((2, 2, HALF // 2, WL), bf),
            pltpu.VMEM((2, 2, 2, HALF // 2, WL), bf),
            pltpu.VMEM((2, 2, 2, HALF // 2, WL), bf),
            pltpu.VMEM((2, HALF // 2, WL), bf),
            pltpu.VMEM((2, HALF // 2, WL), bf),
            pltpu.VMEM((2, HALF // 2, WL), bf),
            dma((4,)),
            dma((6,)), dma((6,)),
            dma((NF,)), dma((NF,)),
            dma((2, NF)), dma((2, NF)),
            dma((NF,)), dma,
            dma((NZ,)), dma((NZ,)), dma((NZ,)),
            dma((NX,)), dma((NX + 2,)),
            dma((2, 6)), dma((2, 6)),
        ],
        compiler_params=pltpu.CompilerParams(
            collective_id=ident, has_side_effects=True, vmem_limit_bytes=56 * 1024 * 1024
        ),
    )(kinds, qkv, weight)


def local(qkv, head_kinds, out_weight):
    chip = jnp.arange(NY * HC) // HC == jnp.arange(NY)[:, None]
    counts = jnp.sum(jnp.where(chip, head_kinds, 0), axis=1)
    most, least = jnp.max(counts), jnp.min(counts)
    choices = [
        functools.partial(attention, slots, frees, ident)
        for ident, (slots, frees) in enumerate(SIZES)
    ]
    fits = [(most <= slots) & (HC - least <= frees) for slots, frees in SIZES[:-1]]
    index = functools.reduce(
        lambda rest, n: jnp.where(fits[n], n, rest), reversed(range(len(fits))), len(fits)
    )
    return lax.switch(index, choices, head_kinds, qkv.transpose(1, 0, 2), out_weight)


def solution(mesh):
    placed = (P("frame", None, "head"), P(), P("head", None))
    return jax.shard_map(
        local, mesh=mesh, in_specs=placed, out_specs=P("frame", "head"), check_vma=False
    )
```

time: 145 us -> 124 us (0.86)
  Pallas kernels: 141 us -> 119 us
    pallas_call x1, Pallas kernels: 141 us -> 119 us  [attention(): pl.pallas_call(functools.partial(kernel, slots, frees), out_shape=jax.Sha...]
where the time goes in v3:
time: 124 us
  Pallas kernels  119 us (96%)
  between operations  2.07 us (2%)
  other arithmetic  1.5 us (1%)
    pallas_call x1, Pallas kernels, attention(): pl.pallas_call(functools.partial(kernel, slots, frees), out_shape=jax.Sha...  119 us

profile of v3, /device:TPU:1, one launch (start us, length us, event | category | flops | bytes accessed | tf_op | source)
XLA Modules:
  0.0 124.0 jit_solution(11412143924459760134)
XLA Ops:
  0.0 0.8 select_reduce_fusion
  0.8 0.7 fusion
  3.6 119.6 %conditional.1 = (bf16[1024,384]{1,0:T(8,128)(2,1)S(1)}) conditional(s32[]{:T(128)} %clamp.3, (s32[24]{0:T(128)}, bf16[3,1024,384]{2,1,0:T(8,128)(2,1)}, bf16[384,3072]{1,0:T(8,128)(2,1)}) %tuple.32, (s32[24]{0:T(128)}, bf16[3,1024,384]{2,1,0:T(8,128)(2,1)}, bf16[384,3072]{1,0:T(8,128)(2,1)}) %tuple.33, ...), branch_computations={%region_3.4_spmd, %region_4.5_spmd, %region_5.6_spmd, %region_6.7_... | conditional | bytes 8 | solution.py:513
  3.6 119.3 %branch_0_fun.1 = bf16[1024,384]{1,0:T(8,128)(2,1)S(1)} custom-call(s32[24]{0:T(128)} %get-tuple-element.35.kinds, bf16[3,1024,384]{2,1,0:T(8,128)(2,1)} %get-tuple-element.40.qkv_in, bf16[384,3072]{1,0:T(8,128)(2,1)} %get-tuple-element.62.weight), custom_call_target="tpu_custom_call" | custom-call | tf_op jit(solution)/shard_map/cond/branch_0_fun/pallas_call | solution.py:459
  123.2 0.9 copy.20
  (1 shorter events, 0.0 us)

commit v4 on v3

--- a/solution.py
+++ b/solution.py
@@ -501,15 +501,13 @@
 def local(qkv, head_kinds, out_weight):
     chip = jnp.arange(NY * HC) // HC == jnp.arange(NY)[:, None]
     counts = jnp.sum(jnp.where(chip, head_kinds, 0), axis=1)
-    most, least = jnp.max(counts), jnp.min(counts)
+    more = jnp.maximum(counts - SIZES[0][0], 0)[:, None]
+    fewer = jnp.maximum(HC - SIZES[0][1] - counts, 0)[None, :]
+    index = jnp.max(jnp.where((more > 1) | (fewer > 1), len(SIZES) - 1, 2 * more + fewer))
     choices = [
         functools.partial(attention, slots, frees, ident)
         for ident, (slots, frees) in enumerate(SIZES)
     ]
-    fits = [(most <= slots) & (HC - least <= frees) for slots, frees in SIZES[:-1]]
-    index = functools.reduce(
-        lambda rest, n: jnp.where(fits[n], n, rest), reversed(range(len(fits))), len(fits)
-    )
     return lax.switch(index, choices, head_kinds, qkv.transpose(1, 0, 2), out_weight)
 
 

time: 124 us -> 134 us (1.081)
  Pallas kernels: 119 us -> 130 us
  between operations: 2.07 us -> 0.67 us
    pallas_call x1, Pallas kernels: 119 us -> 130 us  [attention(): pl.pallas_call(functools.partial(kernel, slots, frees), out_shape=jax.Sha...]
where the time goes in v4:
time: 134 us
  Pallas kernels  130 us (97%)
  other arithmetic  1.5 us (1%)
    pallas_call x1, Pallas kernels, attention(): pl.pallas_call(functools.partial(kernel, slots, frees), out_shape=jax.Sha...  130 us

profile of v4, /device:TPU:1, one launch (start us, length us, event | category | flops | bytes accessed | tf_op | source)
XLA Modules:
  0.0 133.6 jit_solution(4205175316169374685)
XLA Ops:
  0.0 0.8 select_reduce_fusion.1
  0.8 0.7 select_reduce_fusion
  2.2 130.5 %conditional.1 = (bf16[1024,384]{1,0:T(8,128)(2,1)S(1)}) conditional(s32[]{:T(128)} %clamp.3, (s32[24]{0:T(128)}, bf16[3,1024,384]{2,1,0:T(8,128)(2,1)}, bf16[384,3072]{1,0:T(8,128)(2,1)}) %tuple.33, (s32[24]{0:T(128)}, bf16[3,1024,384]{2,1,0:T(8,128)(2,1)}, bf16[384,3072]{1,0:T(8,128)(2,1)}) %tuple.34, ...), branch_computations={%region_2.3_spmd, %region_3.4_spmd, %region_4.5_spmd, %region_5.6_... | conditional | bytes 8 | solution.py:511
  2.2 130.3 %branch_1_fun.1 = bf16[1024,384]{1,0:T(8,128)(2,1)S(1)} custom-call(s32[24]{0:T(128)} %get-tuple-element.44.kinds, bf16[3,1024,384]{2,1,0:T(8,128)(2,1)} %get-tuple-element.45.qkv_in, bf16[384,3072]{1,0:T(8,128)(2,1)} %get-tuple-element.63.weight), custom_call_target="tpu_custom_call" | custom-call | tf_op jit(solution)/shard_map/cond/branch_1_fun/pallas_call | solution.py:459
  132.7 0.9 copy.20
  (3 shorter events, 0.0 us)
